TPU v7x, 32 devices: a whole 2x2x4 slice. The times are simulated.
32 devices in a mesh: slab: 8 (over z, y), grp: 4 (over x, core).
Axes of the slice: x: 2, y: 2, z: 4, core: 2. Of those that a mesh axis runs over, the one named last changes fastest.
Arguments:
- velocity: float32 [3, 4096], P(None, ('slab', 'grp')), may hold values from -6 to 6
- grad_shape: float32 [4, 3, 16384], P(None, None, ('slab', 'grp')), may hold values from -3 to 3
- element_nodes: int32 [4, 16384], P(None, ('slab', 'grp')), may hold values from 0 to 575
- packet_element: int32 [8192], P(('slab', 'grp')), may hold values from 0 to 511
- dest_slab: int32 [8192], P(('slab', 'grp')), may hold values from 0 to 7, as said below
- live_count: int32 [32], P(('slab', 'grp')), may hold values from 64 to 256, as said below
- entangle: int32 [8192, 256], P(('slab', 'grp')), may hold values from 1 to 8
- conform: float32 [8192, 6, 256], P(('slab', 'grp')), may hold values from -6 to 6
Outputs:
- deformed: float32 [8192, 6, 256], P(('slab', 'grp'))
- nodal_force: float32 [3, 4096], P(None, ('slab', 'grp'))
- arrived: float32 [2, 1024, 6, 256], P(None, ('slab', 'grp'))
Inputs may be any that keep to these rules, and one draw needn't show every extreme that they name: `dest_slab`: packets in dead slots keep their own slab; a live packet goes to its own slab or one of the two next to it; from each device at most 32 packets go to each neighbouring slab, and that many in some devices of every draw. `live_count`: at least 64 live slots on each device, all slots on some.
All inputs are finite; a program needn't handle non-finite values.
Results may differ from a plain program's by a relative error of at most 0.000088.
Values sent between devices are 32-bit elements; how exact they have to be, the bound alone decides.
A program may use at most 64 MiB of HBM per device.

v0:
```python
import jax
import jax.numpy as jnp
from jax import lax
from jax.sharding import PartitionSpec as P

HALO = 64
MOVE = 32


DT = 0.1
TAU = 1.0
PAIRS = ((0, 0), (1, 1), (2, 2), (0, 1), (0, 2), (1, 2))
IDENTITY = (1.0, 1.0, 1.0, 0.0, 0.0, 0.0)
SYMMETRY = ((0, 3, 4), (3, 1, 5), (4, 5, 2))


def from_behind(block, axis, distance):
    devices = range(lax.axis_size(axis))
    route = [(i - distance, i) for i in devices if i - distance in devices]
    return lax.ppermute(block, axis, route)


def deform_chains(comps, vel_grad, links):
    rows = (
        (comps[0], comps[3], comps[4]),
        (comps[3], comps[1], comps[5]),
        (comps[4], comps[5], comps[2]),
    )

    def product(first, second):
        return (
            vel_grad[first, 0][:, None] * rows[0][second]
            + vel_grad[first, 1][:, None] * rows[1][second]
            + vel_grad[first, 2][:, None] * rows[2][second]
        )

    relax = DT / (TAU * links)
    result = []
    for index in range(6):
        first, second = PAIRS[index]
        result.append(
            comps[index]
            + DT * (product(first, second) + product(second, first))
            - relax * (comps[index] - IDENTITY[index])
        )
    return jnp.stack(result, 1)


def migrate(deformed, alive_mask, dest_slab):
    my_slab = lax.axis_index("slab")
    slot_count = deformed.shape[0]
    flat_state = deformed.reshape(slot_count, -1)

    def bucket(selected):
        ranks = jnp.cumsum(selected.astype(jnp.int32)) - 1
        one_hot = (
            (ranks[None, :] == jnp.arange(MOVE, dtype=jnp.int32)[:, None]) & selected[None, :]
        ).astype(jnp.float32)
        return jnp.dot(one_hot, flat_state, precision=lax.Precision.HIGHEST)

    upward = bucket(alive_mask & (dest_slab == my_slab + 1))
    downward = bucket(alive_mask & (dest_slab == my_slab - 1))
    from_lower = from_behind(upward, "slab", 1)
    from_upper = from_behind(downward, "slab", -1)
    return jnp.stack([from_lower, from_upper]).reshape(2, MOVE, 6, -1)


def forces(fresh, alive_mask, packet_element, grad_shape, element_nodes, slab_count):
    elem_count = grad_shape.shape[2]
    ident = jnp.array(IDENTITY, jnp.float32)
    stress = (jnp.mean(fresh, 2) - ident[None, :]) * alive_mask[:, None].astype(jnp.float32)
    member_hot = (
        packet_element[:, None] == jnp.arange(elem_count, dtype=jnp.int32)[None, :]
    ).astype(jnp.float32)
    elem_stress = jnp.dot(stress.T, member_hot, precision=lax.Precision.HIGHEST)
    stress_mat = elem_stress[jnp.array(SYMMETRY)]
    elem_force = -jnp.einsum(
        "ije,aje->iae", stress_mat, grad_shape, precision=lax.Precision.HIGHEST
    )
    partial_value = (
        jnp.zeros((3, slab_count + HALO), jnp.float32)
        .at[:, element_nodes.reshape(-1)]
        .add(elem_force.reshape(3, -1))
    )
    rim_force = from_behind(partial_value[:, slab_count:], "slab", 1)
    whole = partial_value[:, :slab_count].at[:, :HALO].add(rim_force)
    return lax.psum_scatter(whole, "grp", scatter_dimension=1, tiled=True)


def shards(
    velocity, grad_shape, element_nodes, packet_element, dest_slab, live_count, entangle, conform
):
    slab_vel = lax.all_gather(velocity, "grp", axis=1, tiled=True)
    slab_count = slab_vel.shape[1]
    next_rows = from_behind(slab_vel[:, :HALO], "slab", -1)
    extended = jnp.concatenate([slab_vel, next_rows], 1)
    node_vel = jnp.take(extended, element_nodes, axis=1)
    vel_grad = jnp.einsum("iae,aje->ije", node_vel, grad_shape, precision=lax.Precision.HIGHEST)
    packet_grad = jnp.take(vel_grad, packet_element, axis=2)
    slot_count = conform.shape[0]
    alive_mask = jnp.arange(slot_count, dtype=jnp.int32) < live_count[0]
    comps = [conform[:, index, :] for index in range(6)]
    fresh = deform_chains(comps, packet_grad, entangle.astype(jnp.float32))
    deformed = jnp.where(alive_mask[:, None, None], fresh, 0.0)
    nodal_force = forces(fresh, alive_mask, packet_element, grad_shape, element_nodes, slab_count)
    arrived = migrate(deformed, alive_mask, dest_slab)
    return (deformed, nodal_force, arrived)


def solution(mesh):
    in_specs = (
        P(None, ("slab", "grp")),
        P(None, None, ("slab", "grp")),
        P(None, ("slab", "grp")),
        P(("slab", "grp")),
        P(("slab", "grp")),
        P(("slab", "grp")),
        P(("slab", "grp"), None),
        P(("slab", "grp"), None, None),
    )
    out_specs = (
        P(("slab", "grp"), None, None),
        P(None, ("slab", "grp")),
        P(None, ("slab", "grp"), None, None),
    )
    return jax.shard_map(shards, mesh=mesh, in_specs=in_specs, out_specs=out_specs, check_vma=False)
```

profile of v0, /device:TPU:9, one launch (start us, length us, event | category | flops | bytes accessed | tf_op | source)
XLA Modules:
  0.0 125.8 jit_solution(13318965799859459716)
XLA Ops:
  7.2 5.8 %all_gather.3 = f32[3,512]{1,0:T(4,128)S(1)} all-gather(f32[3,128]{1,0:T(4,128)} %param.12), channel_id=1, replica_groups=mesh['slab'=8,'grp'=4] {'grp'}, dimensions={1}, use_global_device_ids=true | all-gather | bytes 7680 | tf_op jit(solution)/shard_map/all_gather | solution.py:93
  13.0 3.0 %collective-permute-start = (f32[3,64]{1,0:T(4,128)S(1)}, f32[3,64]{1,0:T(4,128)S(1)}, u32[]{:S(2)}, u32[]{:S(2)}) collective-permute-start(f32[3,64]{1,0:T(4,128)S(1)} %slice.144), channel_id=1, source_target_pairs={{4,0},{8,4},{12,8},{16,12},{20,16},{24,20},{28,24},{5,1},{9,5},{13... | collective-permute-start | bytes 2312 | tf_op jit(solution)/shard_map/ppermute | solution.py:20
  16.0 0.7 fusion.65
  16.7 0.7 compare_and_fusion
  17.4 0.7 compare_select_fusion.2
  18.1 0.7 compare_and_fusion.3
  18.8 1.1 copy.44
  20.2 1.5 %fusion.73 = (f32[256,1,256]{2,0,1:T(8,128)S(1)}, f32[256,1,256]{2,0,1:T(8,128)S(1)}, f32[256,1,256]{2,0,1:T(8,128)S(1)}, f32[256,1,256]{2,0,1:T(8,128)S(1)}, f3...) fusion(f32[256,6,256]{2,0,1:T(8,128)} %param.19), kind=kLoop, calls=%fused_computation.155 | loop fusion | bytes 3145728 | tf_op jit(solution)/shard_map/slice | solution.py:102
  24.6 0.6 compare_reduce_fusion
  25.5 7.6 %gather_fusion = f32[2048,3]{1,0:T(8,128)} fusion(f32[3,576]{0,1:T(8,128)S(1)} %copy.42, s32[2048]{0:T(1024)S(1)} %broadcast_clamp_fusion), kind=kCustom, calls=%fused_computation | custom fusion | bytes 57344 | tf_op jit(solution)/shard_map/jit(_take)/gather | solution.py:97
  33.1 5.3 %copy.43 = f32[4,512,3]{0,2,1:T(4,128)} copy(f32[4,512,3]{2,1,0:T(8,128)} %bitcast.253) | data formatting | bytes 49152 | tf_op jit(solution)/shard_map/jit(_take)/gather | solution.py:97
  38.4 5.8 %convolution_bitcast_fusion = f32[3,3,512]{1,0,2:T(4,128)} fusion(f32[4,3,512]{1,0,2:T(4,128)S(1)} %copy.44, f32[4,512,3]{0,2,1:T(4,128)} %copy.43, pred[4,512]{0,1:T(8,128)(4,1)S(1)} %copy.41), kind=kOutput, calls=%fused_computation.7 | convolution fusion | flops 227328 | bytes 69632 | tf_op jit(solution)/shard_map/iae,aje->ije/dot_general | solution.py:98
  44.2 3.0 %gather_fusion.1 = f32[256,3,3]{2,1,0:T(4,128)} fusion(f32[3,3,512]{1,0,2:T(4,128)} %convolution_bitcast_fusion, s32[1024]{0:T(1024)S(1)} %get-tuple-element.48), kind=kCustom, calls=%fused_computation.1 | custom fusion | bytes 19456 | tf_op jit(solution)/shard_map/jit(_take)/gather | solution.py:99
  47.2 1.4 %select_bitcast_fusion = f32[3,3,256]{1,0,2:T(4,128)S(1)} fusion(f32[256,3,3]{2,1,0:T(4,128)} %gather_fusion.1, pred[256]{0:T(512)(128)(4,1)S(1)} %compare_and_fusion.3), kind=kLoop, calls=%fused_computation.13 | loop fusion | flops 2304 | bytes 18688 | tf_op jit(solution)/shard_map/jit(_take)/select_n | solution.py:99
  48.6 8.3 %slice_reduce_fusion.2 = (f32[256]{0:T(256)S(1)}, f32[256]{0:T(256)S(1)}, f32[256]{0:T(256)S(1)}, f32[256]{0:T(256)S(1)}, f32[256]{0:T(256)S(1)}, /*index=5*/f32...) fusion(f32[3,3,256]{1,0,2:T(4,128)S(1)} %select_bitcast_fusion), kind=kLoop, calls=%fused_computation.107 | loop fusion | bytes 18432 | tf_op jit(solution)/shard_map/slice | solution.py:32
  58.0 1.3 %fusion.72 = (f32[256,6]{0,1:T(8,128)S(1)}, f32[256,6,256]{0,2,1:T(8,128)}) fusion(f32[256,6,256]{0,2,1:T(8,128)S(1)} %bitcast_dynamic-update-slice_fusion, pred[256]{0:T(512)(128)(4,1)S(1)} %get-tuple-element.49), kind=kLoop, calls=%fused_computation.154 | loop fusion | flops 784896 | bytes 3152128 | tf_op jit(solution)/shard_map/reduce_sum | solution.py:71
  60.2 1.4 %copy.51 = f32[3,3,512]{1,0,2:T(4,128)} copy(f32[3,3,512]{2,1,0:T(4,128)S(1)} %reshape.185) | data formatting | bytes 36864 | tf_op jit(solution)/shard_map/gather | solution.py:76
  61.6 5.8 %fusion = f32[3,4,512]{1,0,2:T(4,128)} fusion(f32[3,3,512]{1,0,2:T(4,128)} %copy.51, f32[4,3,512]{1,0,2:T(4,128)S(1)} %copy.44), kind=kOutput, calls=%fused_computation.6 | convolution fusion | flops 227328 | bytes 67584 | tf_op jit(solution)/shard_map/ije,aje->iae/dot_general | solution.py:77
  67.4 1.5 %copy.53 = f32[3,4,512]{2,1,0:T(4,128)S(1)} copy(f32[3,4,512]{1,0,2:T(4,128)} %fusion) | data formatting | bytes 49152 | tf_op jit(solution)/shard_map/neg | solution.py:77
  69.3 11.5 %scatter_custom_fusion = f32[3,576]{0,1:T(8,128)S(1)} fusion(s32[2048]{0:T(1024)S(1)} %bitcast.259, f32[2048,3]{1,0:T(8,128)S(1)} %copy.54, f32[]{:T(128)} %constant.89.clone.1), kind=kCustom, calls=%fused_computation.103 | custom fusion | flops 6144 | bytes 6916 | tf_op jit(solution)/shard_map/scatter-add | solution.py:83
  80.8 0.7 slice.154
  81.6 1.6 %fusion.55 = f32[32,1536]{1,0:T(8,128)} fusion(f32[256,1536]{0,1:T(8,128)S(1)} %bitcast_select_fusion, s32[256]{0:T(256)S(1)} %add_bitcast_fusion.1, pred[256]{0:T(512)(128)(4,1)S(1)} %get-tuple-element.34), kind=kOutput, calls=%fused_computation.120 | convolution fusion | flops 151011328 | bytes 1770752 | tf_op jit(solution)/shard_map/dot_general | solution.py:59
  83.1 2.2 %collective-permute-start.2 = (f32[32,1536]{1,0:T(8,128)}, f32[32,1536]{1,0:T(8,128)}, u32[]{:S(2)}, u32[]{:S(2)}) collective-permute-start(f32[32,1536]{1,0:T(8,128)} %fusion.55), channel_id=1, source_target_pairs={{0,4},{4,8},{8,12},{12,16},{16,20},{20,24},{24,28},{1,5},{5,9},{9,... | collective-permute-start | bytes 589832 | tf_op jit(solution)/shard_map/ppermute | solution.py:20
  85.4 4.1 %collective-permute-start.1 = (f32[3,64]{0,1:T(8,128)S(1)}, f32[3,64]{0,1:T(8,128)S(1)}, u32[]{:S(2)}, u32[]{:S(2)}) collective-permute-start(f32[3,64]{0,1:T(8,128)S(1)} %slice.156), channel_id=1, source_target_pairs={{0,4},{4,8},{8,12},{12,16},{16,20},{20,24},{24,28},{1,5},{5,9},{9,... | collective-permute-start | bytes 2312 | tf_op jit(solution)/shard_map/ppermute | solution.py:20
  89.4 1.6 %fusion.58 = f32[32,1536]{1,0:T(8,128)} fusion(f32[256,1536]{0,1:T(8,128)S(1)} %bitcast_select_fusion, s32[256]{0:T(256)S(1)} %add_bitcast_fusion, pred[256]{0:T(512)(128)(4,1)S(1)} %get-tuple-element.46), kind=kOutput, calls=%fused_computation.122 | convolution fusion | flops 151011328 | bytes 1770752 | tf_op jit(solution)/shard_map/dot_general | solution.py:59
  91.0 2.1 %collective-permute-start.3 = (f32[32,1536]{1,0:T(8,128)}, f32[32,1536]{1,0:T(8,128)S(1)}, u32[]{:S(2)}, u32[]{:S(2)}) collective-permute-start(f32[32,1536]{1,0:T(8,128)} %fusion.58), channel_id=1, source_target_pairs={{4,0},{8,4},{12,8},{16,12},{20,16},{24,20},{28,24},{5,1},{9,5},{13... | collective-permute-start | bytes 589832 | tf_op jit(solution)/shard_map/ppermute | solution.py:20
  93.2 1.3 %fusion.53 = f32[3,512]{0,1:T(8,128)} fusion(f32[3,512]{0,1:T(8,128)} %slice.154, f32[3,64]{0,1:T(8,128)S(1)} %collective-permute-done.1, f32[3,576]{0,1:T(8,128)S(1)} %scatter_custom_fusion, pred[]{:T(512)} %compare_reduce_fusion), kind=kLoop, calls=%fused_computation.116 | loop fusion | flops 384 | bytes 34816 | tf_op jit(solution)/shard_map/scatter-add | solution.py:86
  94.5 1.6 %copy.55 = f32[256,6,256]{2,0,1:T(8,128)} copy(f32[256,6,256]{0,2,1:T(8,128)S(1)} %copy-done) | data formatting | bytes 3145728
  96.1 19.4 %reduce-scatter.2.cloned.1.call-done = f32[3,128]{0,1:T(8,128)} async-done(((f32[3,512]{0,1:T(8,128)}), f32[3,128]{0,1:T(8,128)}) %reduce-scatter.2.cloned.1.call-update) | async-done | bytes 1552 | tf_op jit(solution)/shard_map/reduce_scatter | solution.py:87
  115.4 1.5 %copy.56 = f32[3,128]{1,0:T(4,128)} copy(f32[3,128]{0,1:T(8,128)} %reduce-scatter.2.cloned.1.call-done) | data formatting | bytes 3072
  116.9 1.0 stack.40
  118.1 0.9 copy.57
  (63 shorter events, 5.0 us)
Async XLA Ops:
  7.2 108.3 %reduce-scatter.2.cloned.1.call-start = ((), (), s32[]{:S(2)}) async-start(), calls=%async_computation.1 | async-start | bytes 327680 | tf_op jit(solution)/shard_map/reduce_scatter | solution.py:87
  13.0 12.3 %collective-permute-start = (f32[3,64]{1,0:T(4,128)S(1)}, f32[3,64]{1,0:T(4,128)S(1)}, u32[]{:S(2)}, u32[]{:S(2)}) collective-permute-start(f32[3,64]{1,0:T(4,128)S(1)} %slice.144), channel_id=1, source_target_pairs={{4,0},{8,4},{12,8},{16,12},{20,16},{24,20},{28,24},{5,1},{9,5},{13... | collective-permute-start | bytes 2312 | tf_op jit(solution)/shard_map/ppermute | solution.py:20
  20.1 2.2 %copy-start.4 = (s32[256]{0:T(256)S(1)}, s32[256]{0:T(256)}, u32[]{:S(2)}) copy-start(s32[256]{0:T(256)} %param.16) | copy-start | bytes 3076
  20.2 3.5 %copy-start.2 = (s32[4,512]{1,0:T(4,128)S(1)}, s32[4,512]{1,0:T(4,128)}, u32[]{:S(2)}) copy-start(s32[4,512]{1,0:T(4,128)} %param.14) | copy-start | bytes 24580
  20.2 3.5 %copy-start.5 = (s32[9]{0:T(128)S(1)}, s32[9]{0:T(128)}, u32[]{:S(2)}) copy-start(s32[9]{0:T(128)} %constant.106) | copy-start | bytes 112
  21.6 2.4 %copy-start.1 = (s32[256,256]{1,0:T(8,128)S(1)}, s32[256,256]{1,0:T(8,128)}, u32[]{:S(2)}) copy-start(s32[256,256]{1,0:T(8,128)} %param.18) | copy-start | bytes 786436
  58.0 1.3 %copy-start.3 = (s32[256]{0:T(256)S(1)}, s32[256]{0:T(256)}, u32[]{:S(2)}) copy-start(s32[256]{0:T(256)} %param.15) | copy-start | bytes 3076
  58.0 1.3 %copy-start.6 = (f32[6]{0:T(128)S(1)}, f32[6]{0:T(128)}, u32[]{:S(2)}) copy-start(f32[6]{0:T(128)} %constant.101) | copy-start | bytes 76
  81.6 12.9 %copy-start = (f32[256,6,256]{0,2,1:T(8,128)S(1)}, f32[256,6,256]{0,2,1:T(8,128)}, u32[]{:S(2)}) copy-start(f32[256,6,256]{0,2,1:T(8,128)} %get-tuple-element.38) | copy-start | bytes 4718596
  83.1 33.8 %collective-permute-start.2 = (f32[32,1536]{1,0:T(8,128)}, f32[32,1536]{1,0:T(8,128)}, u32[]{:S(2)}, u32[]{:S(2)}) collective-permute-start(f32[32,1536]{1,0:T(8,128)} %fusion.55), channel_id=1, source_target_pairs={{0,4},{4,8},{8,12},{12,16},{16,20},{20,24},{24,28},{1,5},{5,9},{9,... | collective-permute-start | bytes 589832 | tf_op jit(solution)/shard_map/ppermute | solution.py:20
  85.4 7.8 %collective-permute-start.1 = (f32[3,64]{0,1:T(8,128)S(1)}, f32[3,64]{0,1:T(8,128)S(1)}, u32[]{:S(2)}, u32[]{:S(2)}) collective-permute-start(f32[3,64]{0,1:T(8,128)S(1)} %slice.156), channel_id=1, source_target_pairs={{0,4},{4,8},{8,12},{12,16},{16,20},{20,24},{24,28},{1,5},{5,9},{9,... | collective-permute-start | bytes 2312 | tf_op jit(solution)/shard_map/ppermute | solution.py:20
  91.0 26.9 %collective-permute-start.3 = (f32[32,1536]{1,0:T(8,128)}, f32[32,1536]{1,0:T(8,128)S(1)}, u32[]{:S(2)}, u32[]{:S(2)}) collective-permute-start(f32[32,1536]{1,0:T(8,128)} %fusion.58), channel_id=1, source_target_pairs={{4,0},{8,4},{12,8},{16,12},{20,16},{24,20},{28,24},{5,1},{9,5},{13... | collective-permute-start | bytes 589832 | tf_op jit(solution)/shard_map/ppermute | solution.py:20
Sparse Core Ops, SparseCore 0:
  94.6 20.8 reduce-scatter.1
where the time goes:
time: 128 us; the launch traced here: 126 us
  local copies, waits for them, and re-layouts  38.1 us (30%)
  other arithmetic  20.8 us (16%)
  waiting for transfers between devices  19.4 us (15%)
  matrix products  15.1 us (12%)
  between operations  15.1 us (12%)
  starting transfers between devices  11.5 us (9%)
  blocking collectives  5.77 us (5%)
    reduce_scatter x1, waiting for transfers between devices, forces(): return lax.psum_scatter(whole, 'grp', scatter_dimension=1, tiled=True)  19.4 us
    gather x2, local copies, waits for them, and re-layouts, shards(): node_vel = jnp.take(extended, element_nodes, axis=1)  13 us
    scatter-add x1, other arithmetic, forces(): partial_value = jnp.zeros((3, slab_count + HALO), jnp.float32).at[:, elem...  11.5 us
    ppermute x4, starting transfers between devices, from_behind(): return lax.ppermute(block, axis, route)  11.4 us
    slice x1, local copies, waits for them, and re-layouts, product(): vel_grad[first, 0][:, None] * rows[0][second]  8.33 us
    unnamed x28, local copies, waits for them, and re-layouts  6.1 us
    dot_general x1, matrix products, shards(): jnp.einsum('iae,aje->ije', node_vel, grad_shape, precision=lax.Precision....  5.84 us
    dot_general x1, matrix products, forces(): jnp.einsum('ije,aje->iae', stress_mat, grad_shape, precision=lax.Precisio...  5.8 us
  transfers between devices with their start and end apart: 5, of which 1 were waited for; matrix products, arithmetic and copies ran while one was open for 12% of the time, Pallas kernels for 0%

commit v1 on v0

v1 whole, which is shorter than its diff:
```python
import functools

import jax
import jax.numpy as jnp
from jax import lax
from jax.experimental import pallas as pl
from jax.experimental.pallas import tpu as pltpu
from jax.sharding import PartitionSpec as P

MOVE = 32
DT = 0.1
TAU = 1.0
PAIRS = ((0, 0), (1, 1), (2, 2), (0, 1), (0, 2), (1, 2))
IDENTITY = (1.0, 1.0, 1.0, 0.0, 0.0, 0.0)
SYMMETRY = ((0, 3, 4), (3, 1, 5), (4, 5, 2))
MESH = pl.DeviceIdType.MESH
F32, BF16 = jnp.float32, jnp.bfloat16
ROWS = 16


def halves(x):
    high = x.astype(BF16)
    return high, (x - high.astype(F32)).astype(BF16)


def dot(a, b):
    return jnp.dot(a, b, preferred_element_type=F32)


def deform(comps, grad, relax):
    result = []
    for index, (i, j) in enumerate(PAIRS):
        first = sum(grad[i][k] * comps[SYMMETRY[k][j]] for k in range(3))
        if i == j:
            change = first + first
        else:
            change = first + sum(grad[j][k] * comps[SYMMETRY[k][i]] for k in range(3))
        off = comps[index] - 1.0 if IDENTITY[index] else comps[index]
        result.append(comps[index] + change - relax * off)
    return result


def kernel(
    slabs, group,
    vel_ref, shape_ref, nodes_ref, elem_ref, dest_ref, live_ref, ent_hbm, con_hbm,
    out_ref, force_ref, arr_ref,
    con, ent, relax, table, node_hot, vel_all, vel_mat, grad_rows, grad_cols, sums,
    force_mat, part, landed, rim, bucket_hot, bucket_in, bucket_out,
    local_sem, vel_send, halo_send, vel_recv, part_send, part_recv, rim_send, rim_recv,
    move_send, move_recv,
):
    s, g = lax.axis_index("slab"), lax.axis_index("grp")
    width = vel_ref.shape[1]
    slots, chains = ent_hbm.shape
    elems = nodes_ref.shape[1]
    span = node_hot.shape[0]
    has_next, has_prev = s < slabs - 1, s > 0

    con_copy = pltpu.make_async_copy(con_hbm, con, local_sem.at[0])
    ent_copy = pltpu.make_async_copy(ent_hbm, ent, local_sem.at[1])
    con_copy.start()
    ent_copy.start()

    barrier = pltpu.get_barrier_semaphore()

    def greet(slab, member):
        pl.semaphore_signal(barrier, inc=1, device_id=(slab, member), device_id_type=MESH)

    for off in range(1, group):
        greet(s, lax.rem(g + off, group))

    @pl.when(has_next)
    def _():
        greet(s + 1, g)

        @pl.when(g > 0)
        def _():
            greet(s + 1, 0)

    @pl.when(has_prev)
    def _():
        greet(s - 1, g)

        @pl.when(g == 0)
        def _():
            for member in range(1, group):
                greet(s - 1, member)

    up, down = jnp.where(has_next, 1, 0), jnp.where(has_prev, 1, 0)
    pl.semaphore_wait(barrier, group - 1 + up + down + jnp.where(g == 0, (group - 1) * down, up))

    def vel_copy(slab, member, slot, send, recv):
        return pltpu.make_async_remote_copy(
            vel_ref, vel_all.at[slot], send, recv, device_id=(slab, member), device_id_type=MESH
        )

    for off in range(1, group):
        vel_copy(s, lax.rem(g + off, group), g, vel_send.at[off], vel_recv.at[g]).start()

    @pl.when(has_prev & (g == 0))
    def _():
        for member in range(group):
            vel_copy(s - 1, member, group, halo_send.at[member], vel_recv.at[group]).start()

    vel_all[g] = vel_ref[...]

    @pl.when(jnp.logical_not(has_next))
    def _():
        vel_all[group] = jnp.zeros_like(vel_ref)
        arr_ref[1] = jnp.zeros_like(arr_ref[1])

    @pl.when(jnp.logical_not(has_prev))
    def _():
        arr_ref[0] = jnp.zeros_like(arr_ref[0])

    table[...] = jnp.zeros_like(table)
    for j in range(3):
        high, low = halves(shape_ref[j])
        table[4 * j:4 * j + 4] = high.astype(F32)
        table[16 + 4 * j:20 + 4 * j] = low.astype(F32)
    nodes = nodes_ref[...]
    table[32:36] = (nodes >> 8).astype(F32)
    table[40:44] = (nodes & 255).astype(F32)
    elem_hot = (lax.broadcasted_iota(jnp.int32, (elems, slots), 0) == elem_ref[...]).astype(F32).astype(BF16)
    picked = dot(table[...].astype(BF16), elem_hot)
    shape = picked[0:12] + picked[16:28]
    index = 256.0 * picked[32:36] + picked[40:44]
    node_id = lax.broadcasted_iota(jnp.int32, (span, slots), 0).astype(F32)
    for a in range(4):
        node_hot[:, a * slots:(a + 1) * slots] = (node_id == index[a:a + 1]).astype(F32).astype(BF16)

    live = live_ref[0]
    alive = lax.broadcasted_iota(jnp.int32, (1, slots), 1) < live
    dest = dest_ref[...]
    goes = [jnp.where(alive & (dest == s + step), 1.0, 0.0) for step in (1, -1)]
    both = jnp.concatenate([jnp.broadcast_to(x, (8, slots)) for x in goes], 0)
    before = lax.broadcasted_iota(jnp.int32, (slots, slots), 0) <= lax.broadcasted_iota(jnp.int32, (slots, slots), 1)
    rank = dot(both.astype(BF16), before.astype(F32).astype(BF16))
    place = (lax.broadcasted_iota(jnp.int32, (MOVE, slots), 0) + 1).astype(F32)
    for way in range(2):
        hot = jnp.where(rank[8 * way:8 * way + 1] == place, goes[way], 0.0)
        bucket_hot[way * MOVE:(way + 1) * MOVE] = hot.astype(BF16)

    con_copy.wait()
    ent_copy.wait()
    hot = bucket_hot[...]
    entangled = ent[...].astype(F32)
    relax[...] = DT / (TAU * entangled)
    links = dot(hot, entangled.astype(BF16))
    bucket_in[6] = jnp.where(links > 0.0, DT / (TAU * jnp.maximum(links, 1.0)), 0.0)
    sums[...] = jnp.zeros_like(sums)
    for c in range(6):
        block = con[c]
        high, low = halves(block)
        bucket_in[c] = dot(hot, high) + dot(hot, low)
        off = block - 1.0 if IDENTITY[c] else block
        sums[:, c:c + 1] = jnp.sum(block, 1, keepdims=True)
        sums[:, 8 + c:9 + c] = jnp.sum(relax[...] * off, 1, keepdims=True)
    means = sums[...].T * (1.0 / chains)
    grad_rows[...] = jnp.zeros_like(grad_rows)
    vel_mat[...] = jnp.zeros_like(vel_mat)
    force_mat[...] = jnp.zeros_like(force_mat)

    for off in range(1, group):
        source = lax.rem(g + group - off, group)
        vel_copy(s, source, source, vel_send.at[off], vel_recv.at[source]).wait_recv()

    @pl.when(has_next)
    def _():
        vel_copy(s + 1, 0, group, halo_send.at[0], vel_recv.at[group]).wait_recv()

    for slot in range(group + 1):
        high, low = halves(vel_all[slot])
        vel_mat[0:3, slot * width:(slot + 1) * width] = high.astype(F32)
        vel_mat[8:11, slot * width:(slot + 1) * width] = low.astype(F32)
    node_vel = dot(vel_mat[...].astype(BF16), node_hot[...])
    node_vel = node_vel[0:3] + node_vel[8:11]
    for j in range(3):
        column = sum(
            node_vel[:, a * slots:(a + 1) * slots] * shape[4 * j + a:4 * j + a + 1] for a in range(4)
        )
        grad_rows[3 * j:3 * j + 3] = DT * column
    grads = grad_rows[...]
    columns = grads.T
    grad_cols[...] = columns

    high, low = halves(columns)
    moving = dot(hot, high) + dot(hot, low)
    for way in range(2):
        rows = slice(way * MOVE, (way + 1) * MOVE)
        here = moving[rows]
        grad = [[here[:, 3 * j + i:3 * j + i + 1] for j in range(3)] for i in range(3)]
        fresh = deform([bucket_in[c, rows] for c in range(6)], grad, bucket_in[6, rows])
        for c in range(6):
            bucket_out[way, c] = fresh[c]

    def move(way, slab):
        return pltpu.make_async_remote_copy(
            bucket_out.at[way], arr_ref.at[way], move_send.at[way], move_recv.at[way],
            device_id=(slab, g), device_id_type=MESH,
        )

    @pl.when(has_next)
    def _():
        move(0, s + 1).start()

    @pl.when(has_prev)
    def _():
        move(1, s - 1).start()

    grad = [[grads[3 * j + i:3 * j + i + 1] for j in range(3)] for i in range(3)]
    mean = [means[c:c + 1] for c in range(6)]
    stress = []
    for c, (i, j) in enumerate(PAIRS):
        first = sum(grad[i][k] * mean[SYMMETRY[k][j]] for k in range(3))
        second = sum(grad[j][k] * mean[SYMMETRY[k][i]] for k in range(3))
        value = mean[c] + (first + second) - means[8 + c:9 + c] - IDENTITY[c]
        stress.append(jnp.where(alive, value, 0.0))
    for i in range(3):
        for a in range(4):
            pull = -sum(stress[SYMMETRY[i][j]] * shape[4 * j + a:4 * j + a + 1] for j in range(3))
            high, low = halves(pull)
            force_mat[i:i + 1, a * slots:(a + 1) * slots] = high.astype(F32)
            force_mat[8 + i:9 + i, a * slots:(a + 1) * slots] = low.astype(F32)
    total = lax.dot_general(
        force_mat[...].astype(BF16), node_hot[...], (((1,), (1,)), ((), ())), preferred_element_type=F32
    )
    total = total[0:3] + total[8:11]
    for slot in range(group + 1):
        part[slot] = total[:, slot * width:(slot + 1) * width]

    def part_copy(member, source_slot, landing, send):
        return pltpu.make_async_remote_copy(
            part.at[source_slot], landed.at[landing], send, part_recv.at[landing],
            device_id=(s, member), device_id_type=MESH,
        )

    def rim_copy(slab, landing):
        return pltpu.make_async_remote_copy(
            part.at[group], rim.at[landing], rim_send.at[0], rim_recv.at[landing],
            device_id=(slab, 0), device_id_type=MESH,
        )

    @pl.when(has_next)
    def _():
        rim_copy(s + 1, g).start()

    for off in range(1, group):
        member = lax.rem(g + off, group)
        part_copy(member, member, g, part_send.at[off]).start()

    def chunk(step, carry):
        rows = pl.ds(pl.multiple_of(step * ROWS, ROWS), ROWS)
        here = grad_cols[rows]
        grad = [[here[:, 3 * j + i:3 * j + i + 1] for j in range(3)] for i in range(3)]
        fresh = deform([con[c, rows] for c in range(6)], grad, relax[rows])
        keep = lax.broadcasted_iota(jnp.int32, (ROWS, chains), 0) + step * ROWS < live
        for c in range(6):
            out_ref[c, rows] = jnp.where(keep, fresh[c], 0.0)
        return carry

    lax.fori_loop(0, slots // ROWS, chunk, 0)

    nodal = part[g]
    for off in range(1, group):
        source = lax.rem(g + group - off, group)
        part_copy(source, source, source, part_send.at[off]).wait_recv()
        nodal = nodal + landed[source]
    force_ref[...] = nodal

    @pl.when(has_prev & (g == 0))
    def _():
        more = force_ref[...]
        for member in range(group):
            rim_copy(s - 1, member).wait_recv()
            more = more + rim[member]
        force_ref[...] = more

    @pl.when(has_prev)
    def _():
        move(0, s - 1).wait_recv()
        move(1, s - 1).wait_send()

    @pl.when(has_next)
    def _():
        move(1, s + 1).wait_recv()
        move(0, s + 1).wait_send()
        rim_copy(s + 1, g).wait_send()

    for off in range(1, group):
        member = lax.rem(g + off, group)
        vel_copy(s, member, g, vel_send.at[off], vel_recv.at[g]).wait_send()
        part_copy(member, member, g, part_send.at[off]).wait_send()

    @pl.when(has_prev & (g == 0))
    def _():
        for member in range(group):
            vel_copy(s - 1, member, group, halo_send.at[member], vel_recv.at[group]).wait_send()


def shards(slabs, group, velocity, grad_shape, element_nodes, packet_element, dest_slab, live_count, entangle, conform):
    slots, chains = entangle.shape
    width = velocity.shape[1]
    span = (group + 1) * width
    vmem = pl.BlockSpec(memory_space=pltpu.VMEM)
    smem = pl.BlockSpec(memory_space=pltpu.SMEM)
    hbm = pl.BlockSpec(memory_space=pl.ANY)
    dma = pltpu.SemaphoreType.DMA
    out, force, arrived = pl.pallas_call(
        functools.partial(kernel, slabs, group),
        out_shape=(
            jax.ShapeDtypeStruct((6, slots, chains), F32),
            jax.ShapeDtypeStruct(velocity.shape, F32),
            jax.ShapeDtypeStruct((2, 6, MOVE, chains), F32),
        ),
        in_specs=[vmem, vmem, vmem, vmem, vmem, smem, hbm, hbm],
        out_specs=(vmem, vmem, vmem),
        scratch_shapes=[
            pltpu.VMEM((6, slots, chains), F32),
            pltpu.VMEM((slots, chains), jnp.int32),
            pltpu.VMEM((slots, chains), F32),
            pltpu.VMEM((48, element_nodes.shape[1]), F32),
            pltpu.VMEM((span, 4 * slots), BF16),
            pltpu.VMEM((group + 1, 3, width), F32),
            pltpu.VMEM((16, span), F32),
            pltpu.VMEM((128, slots), F32),
            pltpu.VMEM((slots, 128), F32),
            pltpu.VMEM((slots, 128), F32),
            pltpu.VMEM((16, 4 * slots), F32),
            pltpu.VMEM((group + 1, 3, width), F32),
            pltpu.VMEM((group, 3, width), F32),
            pltpu.VMEM((group, 3, width), F32),
            pltpu.VMEM((2 * MOVE, slots), BF16),
            pltpu.VMEM((7, 2 * MOVE, chains), F32),
            pltpu.VMEM((2, 6, MOVE, chains), F32),
            dma((2,)), dma((group,)), dma((group,)), dma((group + 1,)), dma((group,)), dma((group,)),
            dma((1,)), dma((group,)), dma((2,)), dma((2,)),
        ],
        compiler_params=pltpu.CompilerParams(
            collective_id=0, has_side_effects=True, vmem_limit_bytes=24 * 2**20
        ),
    )(
        velocity, grad_shape.transpose(1, 0, 2), element_nodes, packet_element.reshape(1, slots),
        dest_slab.reshape(1, slots), live_count, entangle, conform.transpose(1, 0, 2),
    )
    return out.transpose(1, 0, 2), force, arrived.transpose(0, 2, 1, 3)


def solution(mesh):
    both = ("slab", "grp")
    in_specs = (
        P(None, both), P(None, None, both), P(None, both), P(both), P(both), P(both),
        P(both, None), P(both, None, None),
    )
    out_specs = (P(both, None, None), P(None, both), P(None, both, None, None))
    body = functools.partial(shards, mesh.shape["slab"], mesh.shape["grp"])
    return jax.shard_map(body, mesh=mesh, in_specs=in_specs, out_specs=out_specs, check_vma=False)
```

time: 128 us -> 27.6 us (0.22); the launches traced: 126 us -> 27.3 us
  local copies, waits for them, and re-layouts: 38.1 us -> 8.29 us
  other arithmetic: 20.8 us -> 0 us
  waiting for transfers between devices: 19.4 us -> 0 us
  Pallas kernels: 0 us -> 17.7 us
  matrix products: 15.1 us -> 0 us
  between operations: 15.1 us -> 1.3 us
  starting transfers between devices: 11.5 us -> 0 us
  blocking collectives: 5.77 us -> 0 us
    reduce_scatter x1 -> x0, waiting for transfers between devices: 19.4 us -> none  [forces(): return lax.psum_scatter(whole, 'grp', scatter_dimension=1, tiled=True)]
    gather x6 -> x0, local copies, waits for them, and re-layouts: 17.9 us -> none  [the longest x2 13 us: shards(): node_vel = jnp.take(extended, element_nodes, axis=1)]
    pallas_call x0 -> x1, Pallas kernels: none -> 17.7 us  [shards(): pl.pallas_call(functools.partial(kernel, slabs, group), out_shape=(jax.Sh...]
    dot_general x5 -> x0, matrix products: 15.1 us -> none  [the longest x1 5.84 us: shards(): jnp.einsum('iae,aje->ije', node_vel, grad_shape, precision=lax.Precision....]
    scatter-add x2 -> x0, other arithmetic: 12.8 us -> none  [the longest x1 11.5 us: forces(): partial_value = jnp.zeros((3, slab_count + HALO), jnp.float32).at[:, elem...]
    ppermute x4 -> x0, starting transfers between devices: 11.4 us -> none  [from_behind(): return lax.ppermute(block, axis, route)]
    slice x5 -> x0, local copies, waits for them, and re-layouts: 10.5 us -> none  [the longest x1 8.33 us: product(): vel_grad[first, 0][:, None] * rows[0][second]]
    all_gather x1 -> x0, blocking collectives: 5.77 us -> none  [shards(): slab_vel = lax.all_gather(velocity, 'grp', axis=1, tiled=True)]
  transfers between devices with their start and end apart: 5 -> 0, of which waited for: 1 -> 0; matrix products, arithmetic and copies ran while one was open for 12% -> 0% of each run, Pallas kernels for 0% -> 0%
where the time goes in v1:
time: 27.6 us; the launch traced here: 27.3 us
  Pallas kernels  17.7 us (64%)
  local copies, waits for them, and re-layouts  8.29 us (30%)
  between operations  1.3 us (5%)
    pallas_call x1, Pallas kernels, shards(): pl.pallas_call(functools.partial(kernel, slabs, group), out_shape=(jax.Sh...  17.7 us
    unnamed x17, local copies, waits for them, and re-layouts  8.29 us

profile of v1, /device:TPU:9, one launch (start us, length us, event | category | flops | bytes accessed | tf_op | source)
XLA Modules:
  0.0 27.3 jit_solution(10744622316225411524)
XLA Ops:
  1.3 0.0 copy-start
  1.3 1.4 %copy-done = f32[256,6,256]{2,0,1:T(8,128)S(1)} copy-done((f32[256,6,256]{2,0,1:T(8,128)S(1)}, f32[256,6,256]{2,0,1:T(8,128)}, u32[]{:S(2)}) %copy-start) | copy-done | bytes 1572888
  2.7 0.0 copy-start.1
  2.7 0.9 %copy-done.1 = s32[256,256]{1,0:T(8,128)S(1)} copy-done((s32[256,256]{1,0:T(8,128)S(1)}, s32[256,256]{1,0:T(8,128)}, u32[]{:S(2)}) %copy-start.1) | copy-done | bytes 262168
  3.6 0.0 copy-start.2
  3.6 0.7 %copy-done.2 = f32[4,3,512]{2,0,1:T(4,128)S(1)} copy-done((f32[4,3,512]{2,0,1:T(4,128)S(1)}, f32[4,3,512]{2,0,1:T(4,128)}, u32[]{:S(2)}) %copy-start.2) | copy-done | bytes 24600
  4.4 0.0 copy-start.3
  4.4 0.7 %copy-done.3 = s32[4,512]{1,0:T(4,128)S(1)} copy-done((s32[4,512]{1,0:T(4,128)S(1)}, s32[4,512]{1,0:T(4,128)}, u32[]{:S(2)}) %copy-start.3) | copy-done | bytes 8216
  5.1 0.0 copy-start.4
  5.1 0.7 %copy-done.4 = f32[3,128]{1,0:T(4,128)S(1)} copy-done((f32[3,128]{1,0:T(4,128)S(1)}, f32[3,128]{1,0:T(4,128)}, u32[]{:S(2)}) %copy-start.4) | copy-done | bytes 1560
  5.8 0.0 copy-start.5
  5.8 0.7 %copy-done.5 = s32[256]{0:T(256)S(1)} copy-done((s32[256]{0:T(256)S(1)}, s32[256]{0:T(256)}, u32[]{:S(2)}) %copy-start.5) | copy-done | bytes 1048
  6.4 0.0 copy-start.6
  6.4 0.7 %copy-done.6 = s32[256]{0:T(256)S(1)} copy-done((s32[256]{0:T(256)S(1)}, s32[256]{0:T(256)}, u32[]{:S(2)}) %copy-start.6) | copy-done | bytes 1048
  7.1 17.7 %shard_map.103 = (f32[6,256,256]{2,1,0:T(8,128)S(1)}, f32[3,128]{1,0:T(4,128)S(1)}, f32[2,6,32,256]{3,2,1,0:T(8,128)S(1)}) custom-call(f32[3,128]{1,0:T(4,128)S(1)} %copy-done.4, f32[3,4,512]{2,1,0:T(4,128)S(1)} %bitcast.9, s32[4,512]{1,0:T(4,128)S(1)} %copy-done.3, s32[1,256]{1,0:T(1,128)S(1)} %bitcast.10, s32[1,256]{1,0:T(1,128)S(1)} %bitcast.11, ...), custom_call_target="tpu_custom_call" | custom-call | tf_op jit(solution)/shard_map/pallas_call | solution.py:309
  24.8 1.1 %copy.15 = f32[256,6,256]{2,0,1:T(8,128)} copy(f32[256,6,256]{2,0,1:T(8,128)S(1)} %bitcast.6) | data formatting | bytes 3145728
  26.0 0.6 %copy.16 = f32[3,128]{1,0:T(4,128)} copy(f32[3,128]{1,0:T(4,128)S(1)} %get-tuple-element.13) | data formatting | bytes 3072
  26.6 0.7 %copy.17 = f32[2,32,6,256]{3,1,2,0:T(8,128)} copy(f32[2,32,6,256]{3,1,2,0:T(8,128)S(1)} %bitcast.8) | data formatting | bytes 786432
Async XLA Ops:
  1.3 1.4 %copy-start = (f32[256,6,256]{2,0,1:T(8,128)S(1)}, f32[256,6,256]{2,0,1:T(8,128)}, u32[]{:S(2)}) copy-start(f32[256,6,256]{2,0,1:T(8,128)} %param.15) | copy-start | bytes 4718596
  2.7 0.9 %copy-start.1 = (s32[256,256]{1,0:T(8,128)S(1)}, s32[256,256]{1,0:T(8,128)}, u32[]{:S(2)}) copy-start(s32[256,256]{1,0:T(8,128)} %ent_hbm.1) | copy-start | bytes 786436
  3.6 0.7 %copy-start.2 = (f32[4,3,512]{2,0,1:T(4,128)S(1)}, f32[4,3,512]{2,0,1:T(4,128)}, u32[]{:S(2)}) copy-start(f32[4,3,512]{2,0,1:T(4,128)} %param.9) | copy-start | bytes 73732
  4.4 0.7 %copy-start.3 = (s32[4,512]{1,0:T(4,128)S(1)}, s32[4,512]{1,0:T(4,128)}, u32[]{:S(2)}) copy-start(s32[4,512]{1,0:T(4,128)} %nodes_ref.1) | copy-start | bytes 24580
  5.1 0.7 %copy-start.4 = (f32[3,128]{1,0:T(4,128)S(1)}, f32[3,128]{1,0:T(4,128)}, u32[]{:S(2)}) copy-start(f32[3,128]{1,0:T(4,128)} %vel_ref.1) | copy-start | bytes 4612
  5.8 0.7 %copy-start.5 = (s32[256]{0:T(256)S(1)}, s32[256]{0:T(256)}, u32[]{:S(2)}) copy-start(s32[256]{0:T(256)} %param.11) | copy-start | bytes 3076
  6.4 0.7 %copy-start.6 = (s32[256]{0:T(256)S(1)}, s32[256]{0:T(256)}, u32[]{:S(2)}) copy-start(s32[256]{0:T(256)} %param.12) | copy-start | bytes 3076

commit v2 on v1

--- a/solution.py
+++ b/solution.py
@@ -42,9 +42,9 @@
 
 def kernel(
     slabs, group,
-    vel_ref, shape_ref, nodes_ref, elem_ref, dest_ref, live_ref, ent_hbm, con_hbm,
+    vel_ref, shape_hbm, nodes_hbm, elem_hbm, dest_hbm, live_ref, ent_hbm, con_hbm,
     out_ref, force_ref, arr_ref,
-    con, ent, relax, table, node_hot, vel_all, vel_mat, grad_rows, grad_cols, sums,
+    con, ent, shape_ref, nodes_ref, elem_ref, dest_ref, relax, table, node_hot, vel_all, vel_mat, grad_rows, grad_cols, sums,
     force_mat, part, landed, rim, bucket_hot, bucket_in, bucket_out,
     local_sem, vel_send, halo_send, vel_recv, part_send, part_recv, rim_send, rim_recv,
     move_send, move_recv,
@@ -52,14 +52,17 @@
     s, g = lax.axis_index("slab"), lax.axis_index("grp")
     width = vel_ref.shape[1]
     slots, chains = ent_hbm.shape
-    elems = nodes_ref.shape[1]
+    elems = nodes_hbm.shape[1]
     span = node_hot.shape[0]
     has_next, has_prev = s < slabs - 1, s > 0
 
-    con_copy = pltpu.make_async_copy(con_hbm, con, local_sem.at[0])
-    ent_copy = pltpu.make_async_copy(ent_hbm, ent, local_sem.at[1])
-    con_copy.start()
-    ent_copy.start()
+    arrays = (
+        (elem_hbm, elem_ref), (shape_hbm, shape_ref), (nodes_hbm, nodes_ref), (vel_ref, vel_all.at[g]),
+        (dest_hbm, dest_ref), (ent_hbm, ent), (con_hbm, con),
+    )
+    fetches = [pltpu.make_async_copy(a, b, local_sem.at[i]) for i, (a, b) in enumerate(arrays)]
+    for fetch in fetches:
+        fetch.start()
 
     barrier = pltpu.get_barrier_semaphore()
 
@@ -86,34 +89,9 @@
             for member in range(1, group):
                 greet(s - 1, member)
 
-    up, down = jnp.where(has_next, 1, 0), jnp.where(has_prev, 1, 0)
-    pl.semaphore_wait(barrier, group - 1 + up + down + jnp.where(g == 0, (group - 1) * down, up))
-
-    def vel_copy(slab, member, slot, send, recv):
-        return pltpu.make_async_remote_copy(
-            vel_ref, vel_all.at[slot], send, recv, device_id=(slab, member), device_id_type=MESH
-        )
-
-    for off in range(1, group):
-        vel_copy(s, lax.rem(g + off, group), g, vel_send.at[off], vel_recv.at[g]).start()
-
-    @pl.when(has_prev & (g == 0))
-    def _():
-        for member in range(group):
-            vel_copy(s - 1, member, group, halo_send.at[member], vel_recv.at[group]).start()
-
-    vel_all[g] = vel_ref[...]
-
-    @pl.when(jnp.logical_not(has_next))
-    def _():
-        vel_all[group] = jnp.zeros_like(vel_ref)
-        arr_ref[1] = jnp.zeros_like(arr_ref[1])
-
-    @pl.when(jnp.logical_not(has_prev))
-    def _():
-        arr_ref[0] = jnp.zeros_like(arr_ref[0])
-
     table[...] = jnp.zeros_like(table)
+    for fetch in fetches[:3]:
+        fetch.wait()
     for j in range(3):
         high, low = halves(shape_ref[j])
         table[4 * j:4 * j + 4] = high.astype(F32)
@@ -129,6 +107,32 @@
     for a in range(4):
         node_hot[:, a * slots:(a + 1) * slots] = (node_id == index[a:a + 1]).astype(F32).astype(BF16)
 
+    up, down = jnp.where(has_next, 1, 0), jnp.where(has_prev, 1, 0)
+    pl.semaphore_wait(barrier, group - 1 + up + down + jnp.where(g == 0, (group - 1) * down, up))
+
+    def vel_copy(slab, member, slot, send, recv):
+        return pltpu.make_async_remote_copy(
+            vel_ref, vel_all.at[slot], send, recv, device_id=(slab, member), device_id_type=MESH
+        )
+
+    for off in range(1, group):
+        vel_copy(s, lax.rem(g + off, group), g, vel_send.at[off], vel_recv.at[g]).start()
+
+    @pl.when(has_prev & (g == 0))
+    def _():
+        for member in range(group):
+            vel_copy(s - 1, member, group, halo_send.at[member], vel_recv.at[group]).start()
+
+    @pl.when(jnp.logical_not(has_next))
+    def _():
+        vel_all[group] = jnp.zeros(vel_ref.shape, F32)
+        arr_ref[1] = jnp.zeros_like(arr_ref[1])
+
+    @pl.when(jnp.logical_not(has_prev))
+    def _():
+        arr_ref[0] = jnp.zeros_like(arr_ref[0])
+
+    fetches[4].wait()
     live = live_ref[0]
     alive = lax.broadcasted_iota(jnp.int32, (1, slots), 1) < live
     dest = dest_ref[...]
@@ -141,8 +145,8 @@
         hot = jnp.where(rank[8 * way:8 * way + 1] == place, goes[way], 0.0)
         bucket_hot[way * MOVE:(way + 1) * MOVE] = hot.astype(BF16)
 
-    con_copy.wait()
-    ent_copy.wait()
+    fetches[5].wait()
+    fetches[6].wait()
     hot = bucket_hot[...]
     entangled = ent[...].astype(F32)
     relax[...] = DT / (TAU * entangled)
@@ -161,6 +165,7 @@
     vel_mat[...] = jnp.zeros_like(vel_mat)
     force_mat[...] = jnp.zeros_like(force_mat)
 
+    fetches[3].wait()
     for off in range(1, group):
         source = lax.rem(g + group - off, group)
         vel_copy(s, source, source, vel_send.at[off], vel_recv.at[source]).wait_recv()
@@ -298,26 +303,42 @@
             vel_copy(s - 1, member, group, halo_send.at[member], vel_recv.at[group]).wait_send()
 
 
+def pin(x):
+    return pltpu.with_memory_space_constraint(x, pltpu.HBM)
+
+
+def write_out(*refs):
+    sem = refs[6]
+    copies = [pltpu.make_async_copy(refs[i], refs[3 + i], sem.at[i]) for i in range(3)]
+    for copy in copies:
+        copy.start()
+    for copy in copies:
+        copy.wait()
+
+
 def shards(slabs, group, velocity, grad_shape, element_nodes, packet_element, dest_slab, live_count, entangle, conform):
     slots, chains = entangle.shape
     width = velocity.shape[1]
     span = (group + 1) * width
     vmem = pl.BlockSpec(memory_space=pltpu.VMEM)
-    smem = pl.BlockSpec(memory_space=pltpu.SMEM)
-    hbm = pl.BlockSpec(memory_space=pl.ANY)
+    hbm = pl.BlockSpec(memory_space=pltpu.HBM)
     dma = pltpu.SemaphoreType.DMA
-    out, force, arrived = pl.pallas_call(
+    made = pl.pallas_call(
         functools.partial(kernel, slabs, group),
         out_shape=(
             jax.ShapeDtypeStruct((6, slots, chains), F32),
             jax.ShapeDtypeStruct(velocity.shape, F32),
             jax.ShapeDtypeStruct((2, 6, MOVE, chains), F32),
         ),
-        in_specs=[vmem, vmem, vmem, vmem, vmem, smem, hbm, hbm],
+        in_specs=[hbm] * 5 + [pl.BlockSpec(memory_space=pltpu.SMEM)] + [hbm] * 2,
         out_specs=(vmem, vmem, vmem),
         scratch_shapes=[
             pltpu.VMEM((6, slots, chains), F32),
             pltpu.VMEM((slots, chains), jnp.int32),
+            pltpu.VMEM((3, 4, element_nodes.shape[1]), F32),
+            pltpu.VMEM(element_nodes.shape, jnp.int32),
+            pltpu.VMEM((1, slots), jnp.int32),
+            pltpu.VMEM((1, slots), jnp.int32),
             pltpu.VMEM((slots, chains), F32),
             pltpu.VMEM((48, element_nodes.shape[1]), F32),
             pltpu.VMEM((span, 4 * slots), BF16),
@@ -333,16 +354,24 @@
             pltpu.VMEM((2 * MOVE, slots), BF16),
             pltpu.VMEM((7, 2 * MOVE, chains), F32),
             pltpu.VMEM((2, 6, MOVE, chains), F32),
-            dma((2,)), dma((group,)), dma((group,)), dma((group + 1,)), dma((group,)), dma((group,)),
+            dma((7,)), dma((group,)), dma((group,)), dma((group + 1,)), dma((group,)), dma((group,)),
             dma((1,)), dma((group,)), dma((2,)), dma((2,)),
         ],
         compiler_params=pltpu.CompilerParams(
             collective_id=0, has_side_effects=True, vmem_limit_bytes=24 * 2**20
         ),
     )(
-        velocity, grad_shape.transpose(1, 0, 2), element_nodes, packet_element.reshape(1, slots),
-        dest_slab.reshape(1, slots), live_count, entangle, conform.transpose(1, 0, 2),
+        pin(velocity), pin(grad_shape.transpose(1, 0, 2)), pin(element_nodes), pin(packet_element.reshape(1, slots)),
+        pin(dest_slab.reshape(1, slots)), live_count, pin(entangle), pin(conform.transpose(1, 0, 2)),
     )
+    out, force, arrived = pl.pallas_call(
+        write_out,
+        out_shape=[jax.ShapeDtypeStruct(x.shape, x.dtype) for x in made],
+        in_specs=[vmem] * 3,
+        out_specs=[hbm] * 3,
+        scratch_shapes=[dma((3,))],
+        compiler_params=pltpu.CompilerParams(vmem_limit_bytes=8 * 2**20),
+    )(*made)
     return out.transpose(1, 0, 2), force, arrived.transpose(0, 2, 1, 3)
 
 

time: 27.6 us -> 20.7 us (0.75)
  local copies, waits for them, and re-layouts: 8.29 us -> 0 us
  Pallas kernels: 17.7 us -> 19.2 us
    unnamed x17 -> x0, local copies, waits for them, and re-layouts: 8.29 us -> none
    pallas_call x0 -> x1, Pallas kernels: none -> 1.3 us  [shards(): pl.pallas_call(write_out, out_shape=[jax.ShapeDtypeStruct(x.shape, x.dtyp...]
where the time goes in v2:
time: 20.7 us; the launch traced here: 20.5 us
  Pallas kernels  19.2 us (93%)
  between operations  1.29 us (6%)
    pallas_call x1, Pallas kernels, shards(): pl.pallas_call(functools.partial(kernel, slabs, group), out_shape=(jax.Sh...  17.9 us
    pallas_call x1, Pallas kernels, shards(): pl.pallas_call(write_out, out_shape=[jax.ShapeDtypeStruct(x.shape, x.dtyp...  1.3 us

profile of v2, /device:TPU:9, one launch (start us, length us, event | category | flops | bytes accessed | tf_op | source)
XLA Modules:
  0.0 20.5 jit_solution(2168419733471309182)
XLA Ops:
  1.3 17.9 %shard_map.103 = (f32[6,256,256]{2,1,0:T(8,128)S(1)}, f32[3,128]{1,0:T(4,128)S(1)}, f32[2,6,32,256]{3,2,1,0:T(8,128)S(1)}) custom-call(f32[3,128]{1,0:T(4,128)} %vel_ref.1, f32[3,4,512]{2,1,0:T(4,128)} %bitcast.7, s32[4,512]{1,0:T(4,128)} %nodes_hbm.1, s32[1,256]{1,0:T(1,128)} %bitcast.8, s32[1,256]{1,0:T(1,128)} %bitcast.9, s32[1]{0:T(128)S(6)} %copy.11.live_ref, ...), custom_call_target="tpu_custom_call" | custom-call | tf_op jit(solution)/shard_map/pallas_call | solution.py:326
  19.2 1.3 %shard_map.104 = (f32[6,256,256]{2,1,0:T(8,128)}, f32[3,128]{1,0:T(4,128)}, f32[2,6,32,256]{3,2,1,0:T(8,128)}) custom-call(f32[6,256,256]{2,1,0:T(8,128)S(1)} %get-tuple-element.9.refs_0_, f32[3,128]{1,0:T(4,128)S(1)} %get-tuple-element.10.refs_1_, f32[2,6,32,256]{3,2,1,0:T(8,128)S(1)} %get-tuple-element.11.refs_2_), custom_call_target="tpu_custom_call" | custom-call | tf_op jit(solution)/shard_map/pallas_call | solution.py:367

commit v3 on v2

--- a/solution.py
+++ b/solution.py
@@ -16,6 +16,7 @@
 MESH = pl.DeviceIdType.MESH
 F32, BF16 = jnp.float32, jnp.bfloat16
 ROWS = 16
+RAW = 16
 
 
 def halves(x):
@@ -45,9 +46,9 @@
     vel_ref, shape_hbm, nodes_hbm, elem_hbm, dest_hbm, live_ref, ent_hbm, con_hbm,
     out_ref, force_ref, arr_ref,
     con, ent, shape_ref, nodes_ref, elem_ref, dest_ref, relax, table, node_hot, vel_all, vel_mat, grad_rows, grad_cols, sums,
-    force_mat, part, landed, rim, bucket_hot, bucket_in, bucket_out,
+    force_mat, part, landed, rim, bucket_hot, bucket_in, bucket_out, raw_in, grad_out, grad_in,
     local_sem, vel_send, halo_send, vel_recv, part_send, part_recv, rim_send, rim_recv,
-    move_send, move_recv,
+    move_send, move_recv, raw_send, raw_recv, grad_send, grad_recv,
 ):
     s, g = lax.axis_index("slab"), lax.axis_index("grp")
     width = vel_ref.shape[1]
@@ -88,6 +89,72 @@
         def _():
             for member in range(1, group):
                 greet(s - 1, member)
+
+    fetches[4].wait()
+    live = live_ref[0]
+    alive = lax.broadcasted_iota(jnp.int32, (1, slots), 1) < live
+    dest = dest_ref[...]
+    goes = [jnp.where(alive & (dest == s + step), 1.0, 0.0) for step in (1, -1)]
+    both = jnp.concatenate([jnp.broadcast_to(x, (8, slots)) for x in goes], 0)
+    before = lax.broadcasted_iota(jnp.int32, (slots, slots), 0) <= lax.broadcasted_iota(jnp.int32, (slots, slots), 1)
+    rank = dot(both.astype(BF16), before.astype(F32).astype(BF16))
+    place = (lax.broadcasted_iota(jnp.int32, (MOVE, slots), 0) + 1).astype(F32)
+    for way in range(2):
+        hot = jnp.where(rank[8 * way:8 * way + 1] == place, goes[way], 0.0)
+        bucket_hot[way * MOVE:(way + 1) * MOVE] = hot.astype(BF16)
+
+    fetches[5].wait()
+    fetches[6].wait()
+    hot = bucket_hot[...]
+    entangled = ent[...].astype(F32)
+    links = dot(hot, entangled.astype(BF16))
+    picked_relax = jnp.where(links > 0.0, DT / (TAU * jnp.maximum(links, 1.0)), 0.0)
+    for way in range(2):
+        bucket_in[way, 6] = picked_relax[way * MOVE:(way + 1) * MOVE]
+    for c in range(6):
+        high, low = halves(con[c])
+        chosen = dot(hot, high) + dot(hot, low)
+        for way in range(2):
+            bucket_in[way, c] = chosen[way * MOVE:(way + 1) * MOVE]
+
+    up, down = jnp.where(has_next, 1, 0), jnp.where(has_prev, 1, 0)
+    pl.semaphore_wait(barrier, group - 1 + up + down + jnp.where(g == 0, (group - 1) * down, up))
+
+    def vel_copy(slab, member, slot, send, recv):
+        return pltpu.make_async_remote_copy(
+            vel_ref, vel_all.at[slot], send, recv, device_id=(slab, member), device_id_type=MESH
+        )
+
+    for off in range(1, group):
+        vel_copy(s, lax.rem(g + off, group), g, vel_send.at[off], vel_recv.at[g]).start()
+
+    @pl.when(has_prev & (g == 0))
+    def _():
+        for member in range(group):
+            vel_copy(s - 1, member, group, halo_send.at[member], vel_recv.at[group]).start()
+
+    def raw_copy(way, slab):
+        return pltpu.make_async_remote_copy(
+            bucket_in.at[way, :, 0:RAW], raw_in.at[way], raw_send.at[way], raw_recv.at[way],
+            device_id=(slab, g), device_id_type=MESH,
+        )
+
+    @pl.when(has_next)
+    def _():
+        raw_copy(0, s + 1).start()
+
+    @pl.when(has_prev)
+    def _():
+        raw_copy(1, s - 1).start()
+
+    @pl.when(jnp.logical_not(has_next))
+    def _():
+        vel_all[group] = jnp.zeros(vel_ref.shape, F32)
+        arr_ref[1] = jnp.zeros_like(arr_ref[1])
+
+    @pl.when(jnp.logical_not(has_prev))
+    def _():
+        arr_ref[0] = jnp.zeros_like(arr_ref[0])
 
     table[...] = jnp.zeros_like(table)
     for fetch in fetches[:3]:
@@ -107,56 +174,10 @@
     for a in range(4):
         node_hot[:, a * slots:(a + 1) * slots] = (node_id == index[a:a + 1]).astype(F32).astype(BF16)
 
-    up, down = jnp.where(has_next, 1, 0), jnp.where(has_prev, 1, 0)
-    pl.semaphore_wait(barrier, group - 1 + up + down + jnp.where(g == 0, (group - 1) * down, up))
-
-    def vel_copy(slab, member, slot, send, recv):
-        return pltpu.make_async_remote_copy(
-            vel_ref, vel_all.at[slot], send, recv, device_id=(slab, member), device_id_type=MESH
-        )
-
-    for off in range(1, group):
-        vel_copy(s, lax.rem(g + off, group), g, vel_send.at[off], vel_recv.at[g]).start()
-
-    @pl.when(has_prev & (g == 0))
-    def _():
-        for member in range(group):
-            vel_copy(s - 1, member, group, halo_send.at[member], vel_recv.at[group]).start()
-
-    @pl.when(jnp.logical_not(has_next))
-    def _():
-        vel_all[group] = jnp.zeros(vel_ref.shape, F32)
-        arr_ref[1] = jnp.zeros_like(arr_ref[1])
-
-    @pl.when(jnp.logical_not(has_prev))
-    def _():
-        arr_ref[0] = jnp.zeros_like(arr_ref[0])
-
-    fetches[4].wait()
-    live = live_ref[0]
-    alive = lax.broadcasted_iota(jnp.int32, (1, slots), 1) < live
-    dest = dest_ref[...]
-    goes = [jnp.where(alive & (dest == s + step), 1.0, 0.0) for step in (1, -1)]
-    both = jnp.concatenate([jnp.broadcast_to(x, (8, slots)) for x in goes], 0)
-    before = lax.broadcasted_iota(jnp.int32, (slots, slots), 0) <= lax.broadcasted_iota(jnp.int32, (slots, slots), 1)
-    rank = dot(both.astype(BF16), before.astype(F32).astype(BF16))
-    place = (lax.broadcasted_iota(jnp.int32, (MOVE, slots), 0) + 1).astype(F32)
-    for way in range(2):
-        hot = jnp.where(rank[8 * way:8 * way + 1] == place, goes[way], 0.0)
-        bucket_hot[way * MOVE:(way + 1) * MOVE] = hot.astype(BF16)
-
-    fetches[5].wait()
-    fetches[6].wait()
-    hot = bucket_hot[...]
-    entangled = ent[...].astype(F32)
     relax[...] = DT / (TAU * entangled)
-    links = dot(hot, entangled.astype(BF16))
-    bucket_in[6] = jnp.where(links > 0.0, DT / (TAU * jnp.maximum(links, 1.0)), 0.0)
     sums[...] = jnp.zeros_like(sums)
     for c in range(6):
         block = con[c]
-        high, low = halves(block)
-        bucket_in[c] = dot(hot, high) + dot(hot, low)
         off = block - 1.0 if IDENTITY[c] else block
         sums[:, c:c + 1] = jnp.sum(block, 1, keepdims=True)
         sums[:, 8 + c:9 + c] = jnp.sum(relax[...] * off, 1, keepdims=True)
@@ -191,26 +212,40 @@
 
     high, low = halves(columns)
     moving = dot(hot, high) + dot(hot, low)
+
+    def entries(here):
+        return [[here[:, 3 * j + i:3 * j + i + 1] for j in range(3)] for i in range(3)]
+
     for way in range(2):
-        rows = slice(way * MOVE, (way + 1) * MOVE)
-        here = moving[rows]
-        grad = [[here[:, 3 * j + i:3 * j + i + 1] for j in range(3)] for i in range(3)]
-        fresh = deform([bucket_in[c, rows] for c in range(6)], grad, bucket_in[6, rows])
+        grad_out[way] = moving[way * MOVE:way * MOVE + RAW]
+        rows = slice(RAW, MOVE)
+        fresh = deform(
+            [bucket_in[way, c, rows] for c in range(6)],
+            entries(moving[way * MOVE + RAW:(way + 1) * MOVE]), bucket_in[way, 6, rows],
+        )
         for c in range(6):
             bucket_out[way, c] = fresh[c]
 
+    def grad_copy(way, slab):
+        return pltpu.make_async_remote_copy(
+            grad_out.at[way], grad_in.at[way], grad_send.at[way], grad_recv.at[way],
+            device_id=(slab, g), device_id_type=MESH,
+        )
+
     def move(way, slab):
         return pltpu.make_async_remote_copy(
-            bucket_out.at[way], arr_ref.at[way], move_send.at[way], move_recv.at[way],
+            bucket_out.at[way], arr_ref.at[way, :, RAW:MOVE], move_send.at[way], move_recv.at[way],
             device_id=(slab, g), device_id_type=MESH,
         )
 
     @pl.when(has_next)
     def _():
+        grad_copy(0, s + 1).start()
         move(0, s + 1).start()
 
     @pl.when(has_prev)
     def _():
+        grad_copy(1, s - 1).start()
         move(1, s - 1).start()
 
     grad = [[grads[3 * j + i:3 * j + i + 1] for j in range(3)] for i in range(3)]
@@ -281,15 +316,28 @@
             more = more + rim[member]
         force_ref[...] = more
 
+    def finish(way, slab):
+        raw_copy(way, slab).wait_recv()
+        grad_copy(way, slab).wait_recv()
+        fresh = deform([raw_in[way, c] for c in range(6)], entries(grad_in[way]), raw_in[way, 6])
+        for c in range(6):
+            arr_ref[way, c, 0:RAW] = fresh[c]
+        move(way, slab).wait_recv()
+
+    def sent(way, slab):
+        raw_copy(way, slab).wait_send()
+        grad_copy(way, slab).wait_send()
+        move(way, slab).wait_send()
+
     @pl.when(has_prev)
     def _():
-        move(0, s - 1).wait_recv()
-        move(1, s - 1).wait_send()
-
-    @pl.when(has_next)
-    def _():
-        move(1, s + 1).wait_recv()
-        move(0, s + 1).wait_send()
+        finish(0, s - 1)
+        sent(1, s - 1)
+
+    @pl.when(has_next)
+    def _():
+        finish(1, s + 1)
+        sent(0, s + 1)
         rim_copy(s + 1, g).wait_send()
 
     for off in range(1, group):
@@ -352,10 +400,13 @@
             pltpu.VMEM((group, 3, width), F32),
             pltpu.VMEM((group, 3, width), F32),
             pltpu.VMEM((2 * MOVE, slots), BF16),
-            pltpu.VMEM((7, 2 * MOVE, chains), F32),
-            pltpu.VMEM((2, 6, MOVE, chains), F32),
+            pltpu.VMEM((2, 7, MOVE, chains), F32),
+            pltpu.VMEM((2, 6, MOVE - RAW, chains), F32),
+            pltpu.VMEM((2, 7, RAW, chains), F32),
+            pltpu.VMEM((2, RAW, 128), F32),
+            pltpu.VMEM((2, RAW, 128), F32),
             dma((7,)), dma((group,)), dma((group,)), dma((group + 1,)), dma((group,)), dma((group,)),
-            dma((1,)), dma((group,)), dma((2,)), dma((2,)),
+            dma((1,)), dma((group,)), dma((2,)), dma((2,)), dma((2,)), dma((2,)), dma((2,)), dma((2,)),
         ],
         compiler_params=pltpu.CompilerParams(
             collective_id=0, has_side_effects=True, vmem_limit_bytes=24 * 2**20

time: 20.7 us -> 17 us (0.82)
  Pallas kernels: 19.2 us -> 15.6 us
    pallas_call x1, Pallas kernels: 17.9 us -> 14.3 us  [shards(): pl.pallas_call(functools.partial(kernel, slabs, group), out_shape=(jax.Sh...]
where the time goes in v3:
time: 17 us; the launch traced here: 16.9 us
  Pallas kernels  15.6 us (92%)
  between operations  1.29 us (8%)
    pallas_call x1, Pallas kernels, shards(): pl.pallas_call(functools.partial(kernel, slabs, group), out_shape=(jax.Sh...  14.3 us
    pallas_call x1, Pallas kernels, shards(): pl.pallas_call(write_out, out_shape=[jax.ShapeDtypeStruct(x.shape, x.dtyp...  1.3 us

profile of v3, /device:TPU:9, one launch (start us, length us, event | category | flops | bytes accessed | tf_op | source)
XLA Modules:
  0.0 16.9 jit_solution(5776455247791868674)
XLA Ops:
  1.3 14.3 %shard_map.103 = (f32[6,256,256]{2,1,0:T(8,128)S(1)}, f32[3,128]{1,0:T(4,128)S(1)}, f32[2,6,32,256]{3,2,1,0:T(8,128)S(1)}) custom-call(f32[3,128]{1,0:T(4,128)} %vel_ref.1, f32[3,4,512]{2,1,0:T(4,128)} %bitcast.7, s32[4,512]{1,0:T(4,128)} %nodes_hbm.1, s32[1,256]{1,0:T(1,128)} %bitcast.8, s32[1,256]{1,0:T(1,128)} %bitcast.9, s32[1]{0:T(128)S(6)} %copy.11.live_ref, ...), custom_call_target="tpu_custom_call" | custom-call | tf_op jit(solution)/shard_map/pallas_call | solution.py:374
  15.6 1.3 %shard_map.104 = (f32[6,256,256]{2,1,0:T(8,128)}, f32[3,128]{1,0:T(4,128)}, f32[2,6,32,256]{3,2,1,0:T(8,128)}) custom-call(f32[6,256,256]{2,1,0:T(8,128)S(1)} %get-tuple-element.9.refs_0_, f32[3,128]{1,0:T(4,128)S(1)} %get-tuple-element.10.refs_1_, f32[2,6,32,256]{3,2,1,0:T(8,128)S(1)} %get-tuple-element.11.refs_2_), custom_call_target="tpu_custom_call" | custom-call | tf_op jit(solution)/shard_map/pallas_call | solution.py:418

commit v4 on v3

--- a/solution.py
+++ b/solution.py
@@ -102,59 +102,6 @@
     for way in range(2):
         hot = jnp.where(rank[8 * way:8 * way + 1] == place, goes[way], 0.0)
         bucket_hot[way * MOVE:(way + 1) * MOVE] = hot.astype(BF16)
-
-    fetches[5].wait()
-    fetches[6].wait()
-    hot = bucket_hot[...]
-    entangled = ent[...].astype(F32)
-    links = dot(hot, entangled.astype(BF16))
-    picked_relax = jnp.where(links > 0.0, DT / (TAU * jnp.maximum(links, 1.0)), 0.0)
-    for way in range(2):
-        bucket_in[way, 6] = picked_relax[way * MOVE:(way + 1) * MOVE]
-    for c in range(6):
-        high, low = halves(con[c])
-        chosen = dot(hot, high) + dot(hot, low)
-        for way in range(2):
-            bucket_in[way, c] = chosen[way * MOVE:(way + 1) * MOVE]
-
-    up, down = jnp.where(has_next, 1, 0), jnp.where(has_prev, 1, 0)
-    pl.semaphore_wait(barrier, group - 1 + up + down + jnp.where(g == 0, (group - 1) * down, up))
-
-    def vel_copy(slab, member, slot, send, recv):
-        return pltpu.make_async_remote_copy(
-            vel_ref, vel_all.at[slot], send, recv, device_id=(slab, member), device_id_type=MESH
-        )
-
-    for off in range(1, group):
-        vel_copy(s, lax.rem(g + off, group), g, vel_send.at[off], vel_recv.at[g]).start()
-
-    @pl.when(has_prev & (g == 0))
-    def _():
-        for member in range(group):
-            vel_copy(s - 1, member, group, halo_send.at[member], vel_recv.at[group]).start()
-
-    def raw_copy(way, slab):
-        return pltpu.make_async_remote_copy(
-            bucket_in.at[way, :, 0:RAW], raw_in.at[way], raw_send.at[way], raw_recv.at[way],
-            device_id=(slab, g), device_id_type=MESH,
-        )
-
-    @pl.when(has_next)
-    def _():
-        raw_copy(0, s + 1).start()
-
-    @pl.when(has_prev)
-    def _():
-        raw_copy(1, s - 1).start()
-
-    @pl.when(jnp.logical_not(has_next))
-    def _():
-        vel_all[group] = jnp.zeros(vel_ref.shape, F32)
-        arr_ref[1] = jnp.zeros_like(arr_ref[1])
-
-    @pl.when(jnp.logical_not(has_prev))
-    def _():
-        arr_ref[0] = jnp.zeros_like(arr_ref[0])
 
     table[...] = jnp.zeros_like(table)
     for fetch in fetches[:3]:
@@ -173,6 +120,59 @@
     node_id = lax.broadcasted_iota(jnp.int32, (span, slots), 0).astype(F32)
     for a in range(4):
         node_hot[:, a * slots:(a + 1) * slots] = (node_id == index[a:a + 1]).astype(F32).astype(BF16)
+
+    fetches[5].wait()
+    fetches[6].wait()
+    hot = bucket_hot[...]
+    entangled = ent[...].astype(F32)
+    links = dot(hot, entangled.astype(BF16))
+    picked_relax = jnp.where(links > 0.0, DT / (TAU * jnp.maximum(links, 1.0)), 0.0)
+    for way in range(2):
+        bucket_in[way, 6] = picked_relax[way * MOVE:(way + 1) * MOVE]
+    for c in range(6):
+        high, low = halves(con[c])
+        chosen = dot(hot, high) + dot(hot, low)
+        for way in range(2):
+            bucket_in[way, c] = chosen[way * MOVE:(way + 1) * MOVE]
+
+    up, down = jnp.where(has_next, 1, 0), jnp.where(has_prev, 1, 0)
+    pl.semaphore_wait(barrier, group - 1 + up + down + jnp.where(g == 0, (group - 1) * down, up))
+
+    def vel_copy(slab, member, slot, send, recv):
+        return pltpu.make_async_remote_copy(
+            vel_ref, vel_all.at[slot], send, recv, device_id=(slab, member), device_id_type=MESH
+        )
+
+    for off in range(1, group):
+        vel_copy(s, lax.rem(g + off, group), g, vel_send.at[off], vel_recv.at[g]).start()
+
+    @pl.when(has_prev & (g == 0))
+    def _():
+        for member in range(group):
+            vel_copy(s - 1, member, group, halo_send.at[member], vel_recv.at[group]).start()
+
+    def raw_copy(way, slab):
+        return pltpu.make_async_remote_copy(
+            bucket_in.at[way, :, 0:RAW], raw_in.at[way], raw_send.at[way], raw_recv.at[way],
+            device_id=(slab, g), device_id_type=MESH,
+        )
+
+    @pl.when(has_next)
+    def _():
+        raw_copy(0, s + 1).start()
+
+    @pl.when(has_prev)
+    def _():
+        raw_copy(1, s - 1).start()
+
+    @pl.when(jnp.logical_not(has_next))
+    def _():
+        vel_all[group] = jnp.zeros(vel_ref.shape, F32)
+        arr_ref[1] = jnp.zeros_like(arr_ref[1])
+
+    @pl.when(jnp.logical_not(has_prev))
+    def _():
+        arr_ref[0] = jnp.zeros_like(arr_ref[0])
 
     relax[...] = DT / (TAU * entangled)
     sums[...] = jnp.zeros_like(sums)
@@ -322,7 +322,6 @@
         fresh = deform([raw_in[way, c] for c in range(6)], entries(grad_in[way]), raw_in[way, 6])
         for c in range(6):
             arr_ref[way, c, 0:RAW] = fresh[c]
-        move(way, slab).wait_recv()
 
     def sent(way, slab):
         raw_copy(way, slab).wait_send()
@@ -332,11 +331,19 @@
     @pl.when(has_prev)
     def _():
         finish(0, s - 1)
+
+    @pl.when(has_next)
+    def _():
+        finish(1, s + 1)
+
+    @pl.when(has_prev)
+    def _():
+        move(0, s - 1).wait_recv()
         sent(1, s - 1)
 
     @pl.when(has_next)
     def _():
-        finish(1, s + 1)
+        move(1, s + 1).wait_recv()
         sent(0, s + 1)
         rim_copy(s + 1, g).wait_send()
 

time: 17 us -> 17 us (level)
  no operation moved by 1% of the time
where the time goes in v4:
time: 17 us; the launch traced here: 16.9 us
  Pallas kernels  15.6 us (92%)
  between operations  1.29 us (8%)
    pallas_call x1, Pallas kernels, shards(): pl.pallas_call(functools.partial(kernel, slabs, group), out_shape=(jax.Sh...  14.3 us
    pallas_call x1, Pallas kernels, shards(): pl.pallas_call(write_out, out_shape=[jax.ShapeDtypeStruct(x.shape, x.dtyp...  1.3 us

profile of v4, /device:TPU:9, one launch (start us, length us, event | category | flops | bytes accessed | tf_op | source)
XLA Modules:
  0.0 16.9 jit_solution(17667193162225713656)
XLA Ops:
  1.3 14.3 %shard_map.103 = (f32[6,256,256]{2,1,0:T(8,128)S(1)}, f32[3,128]{1,0:T(4,128)S(1)}, f32[2,6,32,256]{3,2,1,0:T(8,128)S(1)}) custom-call(f32[3,128]{1,0:T(4,128)} %vel_ref.1, f32[3,4,512]{2,1,0:T(4,128)} %bitcast.7, s32[4,512]{1,0:T(4,128)} %nodes_hbm.1, s32[1,256]{1,0:T(1,128)} %bitcast.8, s32[1,256]{1,0:T(1,128)} %bitcast.9, s32[1]{0:T(128)S(6)} %copy.11.live_ref, ...), custom_call_target="tpu_custom_call" | custom-call | tf_op jit(solution)/shard_map/pallas_call | solution.py:381
  15.6 1.3 %shard_map.104 = (f32[6,256,256]{2,1,0:T(8,128)}, f32[3,128]{1,0:T(4,128)}, f32[2,6,32,256]{3,2,1,0:T(8,128)}) custom-call(f32[6,256,256]{2,1,0:T(8,128)S(1)} %get-tuple-element.9.refs_0_, f32[3,128]{1,0:T(4,128)S(1)} %get-tuple-element.10.refs_1_, f32[2,6,32,256]{3,2,1,0:T(8,128)S(1)} %get-tuple-element.11.refs_2_), custom_call_target="tpu_custom_call" | custom-call | tf_op jit(solution)/shard_map/pallas_call | solution.py:425
